TPU v7x, 512 devices: a whole 4x8x8 slice. The times are simulated.
512 devices in a mesh: ctx: 16 (over z, x_lo), ch: 32 (over x_hi, y, core).
Axes of the slice: x: 4 (x_hi: 2, x_lo: 2; x = x_hi * 2 + x_lo), y: 8, z: 8, core: 2. Of those that a mesh axis runs over, the one named last changes fastest.
Arguments:
- hidden: bfloat16 [4096, 4096], P('ctx', 'ch'), may hold values from -6 to 6
- token_ids: int32 [4096], P('ctx'), may hold values from 0 to 11
- embedding: bfloat16 [12, 4096], P(None, 'ch'), may hold values from -6 to 6
- filters: bfloat16 [16, 256], replicated, may hold values from -0.5 to 0.5
- lengths: int32 [16], replicated, may hold values from 1 to 8, as said below
- cotangent: bfloat16 [4096, 4096], P('ctx', 'ch'), may hold values from -6 to 6
Outputs:
- mixed: bfloat16 [4096, 4096], P('ctx', 'ch')
- hidden_grad: bfloat16 [4096, 4096], P('ctx', 'ch')
- filter_grad: float32 [16, 256], replicated
Inputs may be any that keep to these rules, and one draw needn't show every extreme that they name: Group g's filter keeps its first 32 * lengths[g] taps; in every draw two groups have 8 blocks and one group has 1. `token_ids`: a symbol of the vocabulary.
All inputs are finite; a program needn't handle non-finite values.
Results may differ from a plain program's by a relative error of at most 0.0051.
Values may be sent and summed in bfloat16 or wider, within the bound.
No kernel may reach another device: no remote copies, remote signals or barrier semaphores. Data moves between devices by JAX's collectives and lax.ppermute only.
A program may use at most 64 MiB of HBM per device.

v0:
```python
import math
import jax
import jax.numpy as jnp
from jax import lax
from jax.sharding import PartitionSpec as P

GW = 256
BT = 32


def padded_2(x, sides, width):
    for axis, dim in sides:
        peers, length = (lax.axis_size(axis), x.shape[dim])
        up = [(i, (i + 1) % peers) for i in range(peers - 1)]
        down = [(j, i) for i, j in up]
        last = lax.slice_in_dim(x, length - width, length, axis=dim)
        leading = lax.slice_in_dim(x, 0, width, axis=dim)
        before = lax.ppermute(last, axis, up)
        after = lax.ppermute(leading, axis, down)
        x = jnp.concatenate([before, x, after], axis=dim)
    return x


def pad_taps(taps_rows, row_count):
    zeros_side = jnp.zeros((taps_rows.shape[0], row_count), taps_rows.dtype)
    return jnp.concatenate([zeros_side, taps_rows, zeros_side], axis=1)


def toeplitz_block(padded, offset, row_count):
    start = offset * row_count + 1
    window = padded[:, start : start + 2 * row_count - 1]
    flipped = jnp.concatenate(
        [window[:, ::-1], jnp.zeros((window.shape[0], 1), window.dtype)], axis=1
    )
    tiled = jnp.tile(flipped, (1, row_count))
    cut = tiled[:, row_count - 1 : row_count - 1 + row_count * (2 * row_count - 1)]
    return cut.reshape(window.shape[0], row_count, 2 * row_count - 1)[:, :, :row_count]


def diagonal_sums(product, row_count):
    group_num = product.shape[0]
    widened = jnp.concatenate(
        [product[:, :, ::-1], jnp.zeros((group_num, row_count, row_count), product.dtype)], axis=2
    )
    flat = widened.reshape(group_num, 2 * row_count * row_count)[
        :, : row_count * (2 * row_count - 1)
    ]
    return flat.reshape(group_num, row_count, 2 * row_count - 1).sum(axis=1)


def forward_term(block, source):
    return jnp.einsum("gab,bgc->agc", block, source, preferred_element_type=jnp.float32)


def adjoint_term(block, source):
    return jnp.einsum("gba,bgc->agc", block, source, preferred_element_type=jnp.float32)


def correlate(first_rows, second_rows):
    return jnp.einsum("agc,bgc->gab", first_rows, second_rows, preferred_element_type=jnp.float32)


def own_build(block, items):
    inputs_left, grads_right, grads_here = items
    row_count = block.shape[1]
    return (
        forward_term(block, inputs_left),
        adjoint_term(block, grads_right),
        diagonal_sums(correlate(grads_here, inputs_left), row_count),
    )


def other_build(block, items):
    inputs_right, grads_left, grads_here = items
    row_count = block.shape[1]
    return (
        adjoint_term(block, inputs_right),
        forward_term(block, grads_left),
        diagonal_sums(correlate(inputs_right, grads_here), row_count),
    )


def strand_terms(padded, offset, items, build):
    row_count = items[0].shape[0]
    return build(toeplitz_block(padded, offset, row_count), items)


def add_terms(totals, terms, offset, row_count):
    start = offset * row_count + 1
    return (
        totals[0] + terms[0],
        totals[1] + terms[1],
        totals[2].at[:, start : start + 2 * row_count - 1].add(terms[2]),
    )


def folded_path(ext_inputs, ext_grads, own_pad, other_pad, shape3, reach_blocks, tap_count):
    row_count = shape3[0]
    blocks_in = ext_inputs.reshape((2 * reach_blocks + 1,) + shape3)
    blocks_grad = ext_grads.reshape((2 * reach_blocks + 1,) + shape3)
    zeros_rows = jnp.zeros(shape3, jnp.float32)
    zeros_taps = jnp.zeros((shape3[1], (reach_blocks + 2) * row_count), jnp.float32)
    own_tot = (zeros_rows, zeros_rows, zeros_taps)
    other_tot = (zeros_rows, zeros_rows, zeros_taps)
    grads_here = blocks_grad[reach_blocks]
    for offset in range(reach_blocks + 1):
        own_items = (
            blocks_in[reach_blocks - offset],
            blocks_grad[reach_blocks + offset],
            grads_here,
        )
        own_tot = add_terms(
            own_tot, strand_terms(own_pad, offset, own_items, own_build), offset, row_count
        )
        other_items = (
            blocks_in[reach_blocks + offset],
            blocks_grad[reach_blocks - offset],
            grads_here,
        )
        other_tot = add_terms(
            other_tot, strand_terms(other_pad, offset, other_items, other_build), offset, row_count
        )
    out_rows = own_tot[0] + other_tot[0]
    grad_rows = own_tot[1] + other_tot[1]
    return (
        out_rows,
        grad_rows,
        [
            own_tot[2][:, row_count : row_count + tap_count],
            other_tot[2][:, row_count : row_count + tap_count],
        ],
    )


def on_device(hidden, token_ids, embedding, filters, lengths, cotangent):
    row_count, chan_count = hidden.shape
    group_count, tap_count = filters.shape
    reach_blocks = -(-(tap_count - 1) // row_count)
    group_part = min(chan_count, GW)
    group_num = chan_count // group_part
    shape3 = (row_count, group_num, group_part)
    chan_index = lax.axis_index("ch")
    first_group = chan_index * chan_count // GW
    table_rows = embedding.astype(jnp.float32)
    looked = jnp.zeros((row_count, chan_count), jnp.float32)
    for symbol in range(embedding.shape[0]):
        looked = looked + jnp.where(
            (token_ids == symbol)[:, None], table_rows[symbol][None, :], 0.0
        )
    inputs = (hidden.astype(jnp.float32) + looked).astype(jnp.bfloat16)
    tap_mask = jnp.arange(tap_count, dtype=jnp.int32)[None, :] < (lengths * BT)[:, None]
    masked = jnp.where(tap_mask, filters, jnp.zeros_like(filters))
    own_pad = pad_taps(lax.dynamic_slice_in_dim(masked, first_group, group_num, 0), row_count)
    other_start = group_count - first_group - group_num
    other_pad = pad_taps(
        lax.dynamic_slice_in_dim(masked, other_start, group_num, 0)[::-1], row_count
    )
    ext_inputs = padded_2(inputs, (("ctx", 0),), reach_blocks * row_count)
    ext_grads = padded_2(cotangent, (("ctx", 0),), reach_blocks * row_count)
    out_rows, grad_rows, tap_parts = folded_path(
        ext_inputs, ext_grads, own_pad, other_pad, shape3, reach_blocks, tap_count
    )
    mixed = out_rows.reshape(row_count, chan_count).astype(jnp.bfloat16)
    hidden_grad = grad_rows.reshape(row_count, chan_count).astype(jnp.bfloat16)
    zeros_table = jnp.zeros((group_count, tap_count), jnp.float32)
    table = lax.dynamic_update_slice(zeros_table, tap_parts[0], (first_group, 0))
    table = table + lax.dynamic_update_slice(zeros_table, tap_parts[1][::-1], (other_start, 0))
    summed_table = lax.psum(table, ("ctx", "ch"))
    scale = 1.0 / math.sqrt(row_count * lax.axis_size("ctx") * GW)
    filter_grad = jnp.where(tap_mask, summed_table * scale, jnp.float32(0.0))
    return (mixed, hidden_grad, filter_grad)


def solution(mesh):
    placed = (P("ctx", "ch"), P("ctx"), P(None, "ch"), P(), P(), P("ctx", "ch"))
    return jax.shard_map(
        on_device,
        mesh=mesh,
        in_specs=placed,
        out_specs=(P("ctx", "ch"), P("ctx", "ch"), P()),
        check_vma=False,
    )
```

profile of v0, /device:TPU:1, one launch (start us, length us, event | category | flops | bytes accessed | tf_op | source)
XLA Modules:
  0.0 151.2 jit_solution(8839632538140957376)
XLA Ops:
  0.6 0.7 convert_element_type.28
  1.4 0.7 broadcast_compare_fusion.11
  2.1 0.6 add_convert_fusion
  2.7 1.3 collective-permute-start.1
  4.0 4.6 %collective-permute-start = (bf16[256,128]{1,0:T(8,128)(2,1)S(1)}, bf16[256,128]{1,0:T(8,128)(2,1)S(1)}, u32[]{:S(2)}, u32[]{:S(2)}) collective-permute-start(bf16[256,128]{1,0:T(8,128)(2,1)S(1)} %add_convert_fusion), channel_id=1, source_target_pairs={{0,32},{32,64},{64,96},{96,128},{128,160},{160,192},{192,224},{224... | collective-permute-start | bytes 196616 | tf_op jit(solution)/shard_map/ppermute | solution.py:18
  8.6 4.3 %collective-permute-start.3 = (bf16[256,128]{1,0:T(8,128)(2,1)S(1)}, bf16[256,128]{1,0:T(8,128)(2,1)S(1)}, u32[]{:S(2)}, u32[]{:S(2)}) collective-permute-start(bf16[256,128]{1,0:T(8,128)(2,1)S(1)} %copy-done), channel_id=1, source_target_pairs={{0,32},{32,64},{64,96},{96,128},{128,160},{160,192},{192,224},{224... | collective-permute-start | bytes 196616 | tf_op jit(solution)/shard_map/ppermute | solution.py:18
  12.9 1.3 collective-permute-start.2
  14.2 0.6 copy-done.3
  14.9 0.7 copy-done.2
  17.1 1.5 %slice_reduce_fusion.5 = bf16[130816]{0:T(1024)(128)(2,1)S(1)} fusion(bf16[1,131072]{1,0:T(2,128)(2,1)S(1)} %bitcast.105), kind=kLoop, calls=%fused_computation.19 | loop fusion | bytes 523264 | tf_op jit(solution)/shard_map/slice | solution.py:36
  18.7 0.5 reshape.306
  21.0 1.5 %slice_reduce_fusion.7 = bf16[130816]{0:T(1024)(128)(2,1)S(1)} fusion(bf16[1,131072]{1,0:T(2,128)(2,1)S(1)} %bitcast.106), kind=kLoop, calls=%fused_computation.21 | loop fusion | bytes 523264 | tf_op jit(solution)/shard_map/slice | solution.py:36
  22.5 0.5 reshape.302
  23.6 0.6 compare_reduce_fusion
  24.7 1.5 %slice_reduce_fusion.4 = bf16[130816]{0:T(1024)(128)(2,1)S(1)} fusion(bf16[1,131072]{1,0:T(2,128)(2,1)S(1)} %bitcast.107), kind=kLoop, calls=%fused_computation.18 | loop fusion | bytes 523264 | tf_op jit(solution)/shard_map/slice | solution.py:36
  27.6 0.5 copy.19
  28.1 1.4 slice_reduce_fusion.3
  29.9 0.5 copy.21
  30.5 1.4 slice_reduce_fusion.1
  32.4 0.7 broadcast_select_fusion.1
  33.0 0.7 broadcast_select_fusion
  33.7 1.5 slice_reduce_fusion.6
  35.2 0.4 reshape.308
  35.6 0.4 reshape.304
  36.9 0.5 copy.22
  37.4 1.4 slice_reduce_fusion
  40.0 0.5 copy.20
  40.6 1.4 slice_reduce_fusion.2
  43.4 105.2 %psum.7 = f32[16,256]{1,0:T(8,128)S(1)} all-reduce(f32[16,256]{1,0:T(8,128)S(1)} %add.153), channel_id=1, replica_groups=mesh['ctx'=16,'ch'=32] {'ctx','ch'}, use_global_device_ids=true, to_apply=%region_5.6 | all-reduce | flops 4096 | bytes 32768 | tf_op jit(solution)/shard_map/psum | solution.py:168
  149.0 0.7 multiply_select_fusion
  149.6 0.7 copy.12
  150.4 0.9 fusion.2
  (72 shorter events, 10.4 us)
Async XLA Ops:
  0.6 1.4 copy-start.1
  2.1 6.5 %copy-start = (bf16[256,128]{1,0:T(8,128)(2,1)S(1)}, bf16[256,128]{1,0:T(8,128)(2,1)}, u32[]{:S(2)}) copy-start(bf16[256,128]{1,0:T(8,128)(2,1)} %param.19) | copy-start | bytes 196612
  2.7 33.5 %collective-permute-start.1 = (bf16[256,128]{1,0:T(8,128)(2,1)S(1)}, bf16[256,128]{1,0:T(8,128)(2,1)S(1)}, u32[]{:S(2)}, u32[]{:S(2)}) collective-permute-start(bf16[256,128]{1,0:T(8,128)(2,1)S(1)} %add_convert_fusion), channel_id=1, source_target_pairs={{32,0},{64,32},{96,64},{128,96},{160,128},{192,160},{224,192},{256... | collective-permute-start | bytes 196616 | tf_op jit(solution)/shard_map/ppermute | solution.py:19
  4.0 35.2 %collective-permute-start = (bf16[256,128]{1,0:T(8,128)(2,1)S(1)}, bf16[256,128]{1,0:T(8,128)(2,1)S(1)}, u32[]{:S(2)}, u32[]{:S(2)}) collective-permute-start(bf16[256,128]{1,0:T(8,128)(2,1)S(1)} %add_convert_fusion), channel_id=1, source_target_pairs={{0,32},{32,64},{64,96},{96,128},{128,160},{160,192},{192,224},{224... | collective-permute-start | bytes 196616 | tf_op jit(solution)/shard_map/ppermute | solution.py:18
  8.6 140.0 %collective-permute-start.3 = (bf16[256,128]{1,0:T(8,128)(2,1)S(1)}, bf16[256,128]{1,0:T(8,128)(2,1)S(1)}, u32[]{:S(2)}, u32[]{:S(2)}) collective-permute-start(bf16[256,128]{1,0:T(8,128)(2,1)S(1)} %copy-done), channel_id=1, source_target_pairs={{0,32},{32,64},{64,96},{96,128},{128,160},{160,192},{192,224},{224... | collective-permute-start | bytes 196616 | tf_op jit(solution)/shard_map/ppermute | solution.py:18
  12.9 137.5 %collective-permute-start.2 = (bf16[256,128]{1,0:T(8,128)(2,1)S(1)}, bf16[256,128]{1,0:T(8,128)(2,1)S(1)}, u32[]{:S(2)}, u32[]{:S(2)}) collective-permute-start(bf16[256,128]{1,0:T(8,128)(2,1)S(1)} %copy-done), channel_id=1, source_target_pairs={{32,0},{64,32},{96,64},{128,96},{160,128},{192,160},{224,192},{256... | collective-permute-start | bytes 196616 | tf_op jit(solution)/shard_map/ppermute | solution.py:19
  14.2 0.7 copy-start.3
  14.9 0.7 copy-start.2
where the time goes:
time: 152 us; the launch traced here: 151 us
  blocking collectives  105 us (69%)
  local copies, waits for them, and re-layouts  25.5 us (17%)
  starting transfers between devices  11.4 us (8%)
  other arithmetic  5.19 us (3%)
  matrix products  2.77 us (2%)
    psum x1, blocking collectives, on_device(): summed_table = lax.psum(table, ('ctx', 'ch'))  105 us
    ppermute x2, starting transfers between devices, padded_2(): before = lax.ppermute(last, axis, up)  8.84 us
    unnamed x35, local copies, waits for them, and re-layouts  8.22 us
    slice x4, local copies, waits for them, and re-layouts, toeplitz_block(): tiled[:, row_count - 1:row_count - 1 + row_count * (2 * row_count - 1)]  6.09 us
    slice x4, local copies, waits for them, and re-layouts, diagonal_sums(): widened.reshape(group_num, 2 * row_count * row_count)  5.44 us
  transfers between devices with their start and end apart: 4, of which 0 were waited for; matrix products, arithmetic and copies ran while one was open for 19% of the time, Pallas kernels for 0%

commit v1 on v0

--- a/solution.py
+++ b/solution.py
@@ -165,7 +165,7 @@
     zeros_table = jnp.zeros((group_count, tap_count), jnp.float32)
     table = lax.dynamic_update_slice(zeros_table, tap_parts[0], (first_group, 0))
     table = table + lax.dynamic_update_slice(zeros_table, tap_parts[1][::-1], (other_start, 0))
-    summed_table = lax.psum(table, ("ctx", "ch"))
+    summed_table = jnp.sum(lax.all_gather(table, ("ctx", "ch")), axis=0)
     scale = 1.0 / math.sqrt(row_count * lax.axis_size("ctx") * GW)
     filter_grad = jnp.where(tap_mask, summed_table * scale, jnp.float32(0.0))
     return (mixed, hidden_grad, filter_grad)

time: 152 us -> 870 us (5.72)
  waiting for transfers between devices: 0.01 us -> 801 us
  blocking collectives: 105 us -> 0 us
  between operations: 1.12 us -> 14.5 us
    all_gather x0 -> x1, waiting for transfers between devices: none -> 801 us  [on_device(): summed_table = jnp.sum(lax.all_gather(table, ('ctx', 'ch')), axis=0)]
    psum x1 -> x0, blocking collectives: 105 us -> none  [on_device(): summed_table = lax.psum(table, ('ctx', 'ch'))]
  transfers between devices with their start and end apart: 4 -> 5, of which waited for: 0 -> 1; matrix products, arithmetic and copies ran while one was open for 19% -> 3% of each run, Pallas kernels for 0% -> 0%
where the time goes in v1:
time: 870 us; the launch traced here: 865 us
  waiting for transfers between devices  801 us (92%)
  local copies, waits for them, and re-layouts  24.4 us (3%)
  between operations  14.5 us (2%)
  starting transfers between devices  11.6 us (1%)
  other arithmetic  9.9 us (1%)
    all_gather x1, waiting for transfers between devices, on_device(): summed_table = jnp.sum(lax.all_gather(table, ('ctx', 'ch')), axis=0)  801 us
  transfers between devices with their start and end apart: 5, of which 1 were waited for; matrix products, arithmetic and copies ran while one was open for 3% of the time, Pallas kernels for 0%

profile of v1, /device:TPU:1, one launch (start us, length us, event | category | flops | bytes accessed | tf_op | source)
XLA Modules:
  0.0 864.6 jit_solution(15467340984229295797)
XLA Ops:
  7.2 0.7 convert_element_type.28
  7.9 0.7 broadcast_compare_fusion.11
  8.6 1.4 add_convert_fusion
  10.0 1.3 collective-permute-start.1
  11.3 4.6 collective-permute-start
  15.9 0.6 compare_reduce_fusion
  16.6 1.0 fusion.15
  18.3 0.5 copy.22
  18.9 1.4 slice_reduce_fusion.3
  20.7 0.5 copy.24
  21.2 1.4 slice_reduce_fusion.1
  23.1 0.7 broadcast_select_fusion.1
  23.8 0.7 broadcast_select_fusion
  25.3 0.5 copy.25
  25.8 1.4 slice_reduce_fusion
  28.2 0.5 copy.23
  28.7 1.4 slice_reduce_fusion.2
  31.3 0.6 copy-done.1
  32.0 4.3 collective-permute-start.3
  36.2 1.5 collective-permute-start.2
  39.3 1.5 slice_reduce_fusion.5
  40.8 0.5 reshape.308
  41.7 1.5 slice_reduce_fusion.4
  43.3 0.5 reshape.310
  45.2 1.5 slice_reduce_fusion.7
  46.7 0.5 reshape.304
  47.6 1.5 slice_reduce_fusion.6
  51.0 0.7 copy.15
  51.8 0.9 fusion.2
  52.6 800.5 %all-gather.2.cloned.1.call-done = f32[512,16,256]{2,1,0:T(8,128)} async-done(((f32[1,16,256]{2,1,0:T(8,128)}), f32[512,16,256]{2,1,0:T(8,128)}) %all-gather.2.cloned.1.call-update) | async-done | bytes 8388624 | tf_op jit(solution)/shard_map/all_gather | solution.py:168
  853.2 4.0 reduce_sum.49
  857.1 0.7 multiply_select_fusion
  (75 shorter events, 10.3 us)
Async XLA Ops:
  7.2 17.5 %copy-start = (bf16[256,128]{1,0:T(8,128)(2,1)S(1)}, bf16[256,128]{1,0:T(8,128)(2,1)}, u32[]{:S(2)}) copy-start(bf16[256,128]{1,0:T(8,128)(2,1)} %param.19) | copy-start | bytes 196612
  7.2 846.0 %all-gather.2.cloned.1.call-start = ((), (), s32[]{:S(2)}) async-start(), calls=%async_computation | async-start | bytes 8404992 | tf_op jit(solution)/shard_map/all_gather | solution.py:168
  10.0 14.6 %collective-permute-start.1 = (bf16[256,128]{1,0:T(8,128)(2,1)S(1)}, bf16[256,128]{1,0:T(8,128)(2,1)S(1)}, u32[]{:S(2)}, u32[]{:S(2)}) collective-permute-start(bf16[256,128]{1,0:T(8,128)(2,1)S(1)} %add_convert_fusion), channel_id=1, source_target_pairs={{32,0},{64,32},{96,64},{128,96},{160,128},{192,160},{224,192},{256... | collective-permute-start | bytes 196616 | tf_op jit(solution)/shard_map/ppermute | solution.py:19
  11.3 16.3 %collective-permute-start = (bf16[256,128]{1,0:T(8,128)(2,1)S(1)}, bf16[256,128]{1,0:T(8,128)(2,1)S(1)}, u32[]{:S(2)}, u32[]{:S(2)}) collective-permute-start(bf16[256,128]{1,0:T(8,128)(2,1)S(1)} %add_convert_fusion), channel_id=1, source_target_pairs={{0,32},{32,64},{64,96},{96,128},{128,160},{160,192},{192,224},{224... | collective-permute-start | bytes 196616 | tf_op jit(solution)/shard_map/ppermute | solution.py:18
  20.6 17.1 %copy-start.3 = (s32[16]{0:T(128)S(1)}, s32[16]{0:T(128)}, u32[]{:S(2)}) copy-start(s32[16]{0:T(128)} %param.18) | copy-start | bytes 196
  20.6 17.1 %copy-start.2 = (bf16[16,256]{1,0:T(8,128)(2,1)S(1)}, bf16[16,256]{1,0:T(8,128)(2,1)}, u32[]{:S(2)}) copy-start(bf16[16,256]{1,0:T(8,128)(2,1)} %param.17) | copy-start | bytes 24580
  31.3 0.6 copy-start.1
  32.0 18.9 %collective-permute-start.3 = (bf16[256,128]{1,0:T(8,128)(2,1)S(1)}, bf16[256,128]{1,0:T(8,128)(2,1)S(1)}, u32[]{:S(2)}, u32[]{:S(2)}) collective-permute-start(bf16[256,128]{1,0:T(8,128)(2,1)S(1)} %copy-done), channel_id=1, source_target_pairs={{0,32},{32,64},{64,96},{96,128},{128,160},{160,192},{192,224},{224... | collective-permute-start | bytes 196616 | tf_op jit(solution)/shard_map/ppermute | solution.py:18
  36.2 15.5 %collective-permute-start.2 = (bf16[256,128]{1,0:T(8,128)(2,1)S(1)}, bf16[256,128]{1,0:T(8,128)(2,1)S(1)}, u32[]{:S(2)}, u32[]{:S(2)}) collective-permute-start(bf16[256,128]{1,0:T(8,128)(2,1)S(1)} %copy-done), channel_id=1, source_target_pairs={{32,0},{64,32},{96,64},{128,96},{160,128},{192,160},{224,192},{256... | collective-permute-start | bytes 196616 | tf_op jit(solution)/shard_map/ppermute | solution.py:19
Sparse Core Ops, SparseCore 0:
  32.1 821.0 all-gather.1
